TPU v7x, 32 devices: a whole 2x2x4 slice. The times are simulated.
32 devices in a mesh: gx: 8 (over y, x, core), gy: 4 (over z).
Axes of the slice: x: 2, y: 2, z: 4, core: 2. Of those that a mesh axis runs over, the one named last changes fastest.
Arguments:
- velocity: float32 [3, 512, 128, 128], P(None, 'gx', 'gy'), may hold values from -6 to 6
- inflow: float32 [3, 128, 128], P(None, 'gy'), may hold values from -6 to 6
- azimuth: float32 [32], replicated, may hold values from -3.140625 to 3.140625
- positions: int32 [32, 2], replicated, may hold values from 0 to 511, as said below
- crossings: int32 [32, 6], replicated, may hold values from -1 to 95, as said below
- lag_state: float32 [96, 128], P(('gx', 'gy')), may hold values from -0.5 to 1.5
- lag_rate: float32 [96, 128], P(('gx', 'gy')), may hold values from 0.05 to 0.8
- chord_len: float32 [128], replicated, may hold values from 0.3 to 1.5
- twist_angle: float32 [128], replicated, may hold values from -0.4 to 0.4
Outputs:
- velocity_out: float32 [3, 512, 128, 128], P(None, 'gx', 'gy')
- state_out: float32 [96, 128], P(('gx', 'gy'))
Inputs may be any that keep to these rules, and one draw needn't show every extreme that they name: `positions`: every rotor's hub lies in the tile of its cell, 2 or more cells from both x edges of that tile and at most 15 cells below its upper y edge; a tile holds at most two hubs, and two hubs in one tile differ in x. `crossings`: row t lists the blades 3 r, 3 r + 1, 3 r + 2 of every rotor r whose hub lies in tile t, then of some of the rotors whose hub lies in the tile just before t along y (cyclic, same x), and -1 in the remaining entries at the end. Every blade appears in one or two rows; some rows hold 6 blades.
All inputs are finite; a program needn't handle non-finite values.
Results may differ from a plain program's by a relative error of at most 0.0003.
Values sent between devices are 32-bit elements; how exact they have to be, the bound alone decides.
A program may use at most 128 MiB of HBM per device.

v0:
```python
import math

import jax
import jax.numpy as jnp
from jax import lax
from jax.sharding import PartitionSpec as P

RADIUS = 12
HUB = 15
STEPS = 2


EPSILON = 2.0
SUPPORT = 3.0
TURN_RATE = 0.1
SPIN = 0.25
LIFT_SLOPE = 2.0 * math.pi
FORCE_SCALE = 0.15
ADVECT = 0.5
DIFFUSE = 0.05
PRECISE = lax.Precision.HIGHEST


def padded_2(block, sides, width):
    for axis, dim in sides:
        count = lax.axis_size(axis)
        forward = [(i, i + 1) for i in range(count - 1)]
        forward.append((count - 1, 0))
        backward = [(target, source) for source, target in forward]
        low = lax.ppermute(
            lax.slice_in_dim(block, block.shape[dim] - width, None, axis=dim), axis, forward
        )
        high = lax.ppermute(lax.slice_in_dim(block, 0, width, axis=dim), axis, backward)
        block = jnp.concatenate([low, block, high], axis=dim)
    return block


def taper_kernel(distance):
    square = distance * distance
    taper_term = jnp.maximum(1.0 - square / (SUPPORT * SUPPORT), 0.0)
    return (
        jnp.exp(-square / (EPSILON * EPSILON))
        * taper_term
        * taper_term
        / (EPSILON * math.sqrt(math.pi))
    )


def blade_geometry(blade_ids, azimuth, step_id, sections):
    rotor_ids = blade_ids // 3
    azimuths = (
        azimuth[rotor_ids]
        + TURN_RATE * step_id
        + 2.0 * math.pi / 3.0 * (blade_ids % 3).astype(jnp.float32)
    )
    radius = RADIUS * (jnp.arange(sections, dtype=jnp.float32) + 0.5) / sections
    return (jnp.cos(azimuths), jnp.sin(azimuths), radius)


def window_kernels(cosines, sine_az, radius, depth_z):
    offsets_y = jnp.arange(2 * RADIUS + 7, dtype=jnp.float32) - (RADIUS + 3)
    heights = jnp.arange(depth_z, dtype=jnp.float32)
    kern_y = taper_kernel(offsets_y[None, None, :] - radius[None, :, None] * sine_az[:, None, None])
    kern_z = taper_kernel(
        heights[None, None, :] - HUB - radius[None, :, None] * cosines[:, None, None]
    )
    return (kern_y, kern_z)


def blade_forces(samples, lag_now, rates, cosines, sine_az, radius, chord_len, twist_angle):
    cos_b = cosines[:, None]
    sin_b = sine_az[:, None]
    axial_wind = samples[:, 0]
    tangential = SPIN * radius[None, :] - (samples[:, 1] * cos_b - samples[:, 2] * sin_b)
    magnitude = jnp.sqrt(axial_wind * axial_wind + tangential * tangential + 1.0)
    lift_static = (
        LIFT_SLOPE
        * (axial_wind * jnp.cos(twist_angle) - tangential * jnp.sin(twist_angle))
        / magnitude
    )
    updated = lag_now + rates * (lift_static - lag_now)
    lift_force = FORCE_SCALE * chord_len * updated * magnitude
    forces = jnp.stack(
        [
            -lift_force * tangential,
            lift_force * axial_wind * cos_b,
            -lift_force * axial_wind * sin_b,
        ],
        axis=1,
    )
    return (updated, forces)


def advance_tile(velocity, inflow, body_force, first_col, last_col):
    haloed = padded_2(velocity, (("gx", 1), ("gy", 2)), 1)
    west_edge = jnp.where(first_col, inflow, haloed[:, 0, 1:-1])
    east_edge = jnp.where(last_col, velocity[:, -1], haloed[:, -1, 1:-1])
    x_prev = jnp.concatenate([west_edge[:, None], velocity[:, :-1]], axis=1)
    x_next = jnp.concatenate([velocity[:, 1:], east_edge[:, None]], axis=1)
    y_next = haloed[:, 1:-1, 2:]
    y_prev = haloed[:, 1:-1, :-2]
    z_next = jnp.concatenate([velocity[..., 1:], velocity[..., -1:]], axis=3)
    z_prev = jnp.concatenate([jnp.zeros_like(velocity[..., :1]), velocity[..., :-1]], axis=3)
    neighbours = x_prev + x_next + y_next + y_prev + z_next + z_prev
    return (
        velocity
        + ADVECT * (x_prev - velocity)
        + DIFFUSE * (neighbours - 6.0 * velocity)
        + body_force
    )


def per_device(
    velocity, inflow, azimuth, positions, crossings, lag_state, lag_rate, chord_len, twist_angle
):
    count_x = lax.axis_size("gx")
    count_y = lax.axis_size("gy")
    tile_x = lax.axis_index("gx")
    tile_y = lax.axis_index("gy")
    tile_id = tile_x * count_y + tile_y
    components, width_x, width_y, depth_z = velocity.shape
    own_count, sections = lag_state.shape
    total_y = width_y * count_y
    reach_y = RADIUS + 3
    span_y = 2 * reach_y + 1
    margin = 32
    listed = lax.dynamic_index_in_dim(crossings, tile_id, 0, keepdims=False)
    list_len = listed.shape[0]
    live_slots = jnp.sum((listed >= 0).astype(jnp.int32))
    safe_ids = jnp.maximum(listed, 0)
    rotor_ids = safe_ids // 3
    start_x = positions[rotor_ids, 0] - tile_x * width_x - 2
    start_y = (positions[rotor_ids, 1] - reach_y - tile_y * width_y + margin) % total_y
    kern_x = taper_kernel(jnp.arange(5, dtype=jnp.float32) - 2.0)
    own_ids = tile_id * own_count + jnp.arange(own_count, dtype=jnp.int32)
    first_col = tile_x == 0
    last_col = tile_x == count_x - 1
    lag_now = lag_state
    for step_id in range(STEPS):
        cosines, sine_az, radius = blade_geometry(safe_ids, azimuth, step_id, sections)
        kern_y, kern_z = window_kernels(cosines, sine_az, radius, depth_z)
        padded = jnp.pad(velocity, ((0, 0), (0, 0), (margin, margin), (0, 0)))

        def sample_slot(slot_id, gathered):
            window = lax.dynamic_slice(
                padded, (0, start_x[slot_id], start_y[slot_id], 0), (components, 5, span_y, depth_z)
            )
            flattened = jnp.einsum("i,cijz->cjz", kern_x, window, precision=PRECISE)
            inner_sum = jnp.dot(
                flattened.reshape(-1, depth_z), kern_z[slot_id].T, precision=PRECISE
            )
            inner_sum = inner_sum.reshape(components, span_y, sections)
            sampled = jnp.sum(inner_sum * kern_y[slot_id].T[None], axis=1)
            return lax.dynamic_update_index_in_dim(gathered, sampled, slot_id, 0)

        partial_samples = lax.fori_loop(
            0, live_slots, sample_slot, jnp.zeros((list_len, components, sections), jnp.float32)
        )
        flat_partial = partial_samples.reshape(list_len, components * sections)
        own_cos, own_sin, _ = blade_geometry(own_ids, azimuth, step_id, sections)
        selector = (
            jnp.arange(own_count * lax.axis_size(("gx", "gy")), dtype=jnp.int32)[:, None]
            == listed[None, :]
        ).astype(jnp.float32)
        own_samples = lax.psum_scatter(
            jnp.dot(selector, flat_partial, precision=PRECISE),
            ("gx", "gy"),
            scatter_dimension=0,
            tiled=True,
        )
        lag_now, own_forces = blade_forces(
            own_samples.reshape(own_count, components, sections),
            lag_now,
            lag_rate,
            own_cos,
            own_sin,
            radius,
            chord_len,
            twist_angle,
        )
        row_piece = lax.all_gather(
            own_forces.reshape(own_count, components * sections), ("gx", "gy"), axis=0, tiled=True
        )
        pick_selector = (
            listed[:, None] == jnp.arange(row_piece.shape[0], dtype=jnp.int32)[None, :]
        ).astype(jnp.float32)
        list_forces = jnp.dot(pick_selector, row_piece, precision=PRECISE)
        list_forces = list_forces.reshape(list_len, components, sections)

        def spread_slot(slot_id, force_field):
            weighted = list_forces[slot_id][:, None, :] * kern_y[slot_id].T[None]
            spread = jnp.dot(weighted.reshape(-1, sections), kern_z[slot_id], precision=PRECISE)
            spread = spread.reshape(components, span_y, depth_z)
            block_add = kern_x[None, :, None, None] * spread[:, None]
            corner = (0, start_x[slot_id], start_y[slot_id], 0)
            current = lax.dynamic_slice(force_field, corner, block_add.shape)
            return lax.dynamic_update_slice(force_field, current + block_add, corner)

        force_field = lax.fori_loop(0, live_slots, spread_slot, jnp.zeros_like(padded))
        body_force = force_field[:, :, margin : margin + width_y]
        velocity = advance_tile(velocity, inflow, body_force, first_col, last_col)
    return (velocity, lag_now)


def solution(mesh):
    return jax.shard_map(
        per_device,
        mesh=mesh,
        in_specs=(
            P(None, "gx", "gy", None),
            P(None, "gy", None),
            P(),
            P(),
            P(),
            P(("gx", "gy"), None),
            P(("gx", "gy"), None),
            P(),
            P(),
        ),
        out_specs=(P(None, "gx", "gy", None), P(("gx", "gy"), None)),
        check_vma=False,
    )
```

profile of v0, /device:TPU:0, one launch (start us, length us, event | category | flops | bytes accessed | tf_op | source)
XLA Modules:
  0.0 737.3 jit_solution(18057945476321850158)
XLA Ops:
  9.1 1.3 gather_fusion.2
  13.6 6.8 pad.11
  22.4 57.6 %while.44 = (s32[]{:T(128)}, f32[6,3,128]{2,1,0:T(4,128)S(1)}, s32[]{:T(128)}, s32[6]{0:T(128)}, s32[6]{0:T(128)}, /*index=5*/f32[3,64,96,128]{3,2,1,0:T(8,128)}...) while((s32[]{:T(128)}, f32[6,3,128]{2,1,0:T(4,128)S(1)}, ...), condition=%wide.region_3.4_spmd.clone, body=%wide.region_1.3_spmd.clone.sunk | while | flops 19022268 | bytes 929039 | solution.py:156
  26.1 1.3 dynamic_slice.147
  35.6 1.3 dynamic_slice.147
  45.1 1.3 dynamic_slice.147
  54.6 1.3 dynamic_slice.147
  64.1 1.3 dynamic_slice.147
  73.6 1.3 dynamic_slice.147
  81.8 3.7 copy.43
  85.5 3.8 fusion.147
  89.3 3.7 fusion.148
  94.5 2.6 slice.138
  98.3 105.8 %all-reduce.11.cloned.1.call-done = f32[96,384]{1,0:T(8,128)} async-done(((f32[96,384]{1,0:T(8,128)}), f32[96,384]{1,0:T(8,128)}) %all-reduce.11.cloned.1.call-update) | async-done | bytes 147472
  205.6 69.3 %all-gather = f32[32,3,384]{2,1,0:T(4,128)S(1)} all-gather(f32[1,3,384]{2,1,0:T(4,128)S(1)} %maximum_bitcast_fusion), channel_id=1, replica_groups=mesh['gx'=8,'gy'=4] {'gx','gy'}, dimensions={0}, use_global_device_ids=true | all-gather | bytes 152064 | tf_op jit(solution)/shard_map/all_gather | solution.py:181
  276.7 4.9 broadcast.609.clone
  281.6 67.4 %while.45 = (s32[]{:T(128)}, f32[3,64,96,128]{3,2,1,0:T(8,128)}, s32[]{:T(128)}, s32[6]{0:T(128)}, s32[6]{0:T(128)}, /*index=5*/f32[6,3,128]{2,1,0:T(4,128)S(1)}...) while((s32[]{:T(128)}, f32[3,64,96,128]{3,2,1,0:T(8,128)}, ...), condition=%wide.region_6.7_spmd.clone, body=%wide.region_5.6_spmd.clone.sunk | while | flops 18415548 | bytes 1165627 | solution.py:199
  286.8 1.3 dynamic_slice.153
  290.8 1.9 dynamic_update_slice.24
  297.9 1.3 dynamic_slice.153
  301.9 1.9 dynamic_update_slice.24
  309.0 1.3 dynamic_slice.153
  313.0 1.9 dynamic_update_slice.24
  320.1 1.3 dynamic_slice.153
  324.2 1.9 dynamic_update_slice.24
  335.3 1.9 dynamic_update_slice.24
  346.4 1.9 dynamic_update_slice.24
  349.0 9.3 %copy.55 = f32[3,64,96,128]{3,1,2,0:T(8,128)S(1)} copy(f32[3,64,96,128]{3,2,1,0:T(8,128)} %get-tuple-element.195) | data formatting | bytes 18874368 | tf_op jit(solution)/shard_map/while | solution.py:199
  359.3 2.0 collective-permute-start.3
  361.3 2.7 collective-permute-done.2
  364.0 1.9 collective-permute-done.3
  365.9 8.5 %slice_add_fusion.1 = f32[3,64,32,128]{3,1,2,0:T(8,128)S(1)} fusion(f32[3,64,96,128]{3,1,2,0:T(8,128)S(1)} %copy.55, f32[3,66,1,128]{3,1,2,0:T(8,128)S(1)} %collective-permute-done.3, f32[3,1,32,128]{3,1,2,0:T(1,128)S(1)} %copy-done.13, f32[3,64,32,128]{3,1,2,0:T(8,128)} %copy-done.3, f32[3,1,32,128]{3,1,2,0:T(1,128)} %collective-permute-done, ...), kind=kLoop, calls=%fused_computation.116 | loop fusion | flops 17301504 | bytes 22296576 | tf_op jit(solution)/shard_map/add | solution.py:106
  374.5 1.8 copy.76
  376.3 3.6 fusion.144
  379.9 3.7 fusion.145
  384.2 4.8 pad.12.clone
  389.0 58.6 %while.46 = (s32[]{:T(128)}, f32[6,3,128]{2,1,0:T(4,128)S(1)}, s32[]{:T(128)}, s32[6]{0:T(128)}, s32[6]{0:T(128)}, /*index=5*/f32[3,64,96,128]{3,2,1,0:T(8,128)}...) while((s32[]{:T(128)}, f32[6,3,128]{2,1,0:T(4,128)S(1)}, ...), condition=%wide.region_9.10_spmd.clone, body=%wide.region_7.9_spmd.clone.sunk | while | flops 19022268 | bytes 928527 | solution.py:156
  392.9 1.3 dynamic_slice.158
  402.5 1.3 dynamic_slice.158
  412.2 1.3 dynamic_slice.158
  421.8 1.3 dynamic_slice.158
  431.4 1.3 dynamic_slice.158
  441.1 1.3 dynamic_slice.158
  448.5 2.6 slice.149
  451.9 2.0 collective-permute-start.7
  455.2 114.3 %all-reduce.13.cloned.1.call-done = f32[96,384]{1,0:T(8,128)} async-done(((f32[96,384]{1,0:T(8,128)}), f32[96,384]{1,0:T(8,128)}) %all-reduce.13.cloned.1.call-update) | async-done | bytes 147472
  571.1 69.3 %all-gather.1 = f32[32,3,384]{2,1,0:T(4,128)S(1)} all-gather(f32[1,3,384]{2,1,0:T(4,128)S(1)} %maximum_bitcast_fusion.1), channel_id=1, replica_groups=mesh['gx'=8,'gy'=4] {'gx','gy'}, dimensions={0}, use_global_device_ids=true | all-gather | bytes 152064 | tf_op jit(solution)/shard_map/all_gather | solution.py:181
  642.3 4.9 broadcast.609
  647.1 63.8 %while.47 = (s32[]{:T(128)}, f32[3,64,96,128]{3,2,1,0:T(8,128)}, s32[]{:T(128)}, s32[6]{0:T(128)}, s32[6]{0:T(128)}, /*index=5*/f32[6,3,128]{2,1,0:T(4,128)S(1)}...) while((s32[]{:T(128)}, f32[3,64,96,128]{3,2,1,0:T(8,128)}, ...), condition=%wide.region_12.13_spmd.clone, body=%wide.region_11.12_spmd.clone.sunk | while | flops 18415548 | bytes 1165627 | solution.py:199
  651.7 1.3 dynamic_slice.164
  655.8 1.9 dynamic_update_slice.26
  662.2 1.3 dynamic_slice.164
  666.3 1.9 dynamic_update_slice.26
  672.8 1.3 dynamic_slice.164
  676.9 1.9 dynamic_update_slice.26
  683.3 1.3 dynamic_slice.164
  687.4 1.9 dynamic_update_slice.26
  693.8 1.3 dynamic_slice.164
  697.9 1.9 dynamic_update_slice.26
  704.4 1.3 dynamic_slice.164
  708.5 1.9 dynamic_update_slice.26
  711.0 9.3 %copy.66 = f32[3,64,96,128]{3,1,2,0:T(8,128)S(1)} copy(f32[3,64,96,128]{3,2,1,0:T(8,128)} %get-tuple-element.197) | data formatting | bytes 18874368 | tf_op jit(solution)/shard_map/while | solution.py:199
  720.4 6.6 slice_add_fusion
  727.0 3.5 copy.67
  (283 shorter events, 115.1 us)
Async XLA Ops:
  7.2 3.4 copy-start
  7.2 196.9 %all-reduce.11.cloned.1.call-start = ((), (), s32[]{:S(2)}) async-start(), calls=%async_computation | async-start | bytes 294912
  8.1 267.5 %copy-start.18 = (s32[6]{0:T(128)}, s32[6]{0:T(128)S(1)}, u32[]{:S(2)}) copy-start(s32[6]{0:T(128)S(1)} %get-tuple-element.285) | copy-start | bytes 76
  80.0 1.7 copy-start.7
  80.9 488.6 %all-reduce.13.cloned.1.call-start = ((), (), s32[]{:S(2)}) async-start(), calls=%async_computation.1 | async-start | bytes 294912
  81.8 15.3 %collective-permute-start.1 = (f32[3,1,32,128]{3,1,2,0:T(1,128)S(1)}, f32[3,1,32,128]{3,1,2,0:T(1,128)S(1)}, u32[]{:S(2)}, u32[]{:S(2)}) collective-permute-start(f32[3,1,32,128]{3,1,2,0:T(1,128)S(1)} %bitcast.255), channel_id=1, source_target_pairs={{4,0},{8,4},{12,8},{16,12},{20,16},{24,20},{28,24},{0,28},{5,1},{9... | collective-permute-start | bytes 147464 | tf_op jit(solution)/shard_map/ppermute | solution.py:33
  85.5 272.9 %copy-start.3 = (f32[3,64,32,128]{3,1,2,0:T(8,128)}, f32[3,64,32,128]{3,1,2,0:T(8,128)S(1)}, u32[]{:S(2)}) copy-start(f32[3,64,32,128]{3,1,2,0:T(8,128)S(1)} %copy.43) | copy-start | bytes 9437188
  89.3 3.8 copy-start.2
  89.3 5.0 copy-start.34
  89.3 5.0 copy-start.35
  94.4 110.4 %copy-start.23 = (f32[128]{0:T(128)}, f32[128]{0:T(128)S(1)}, u32[]{:S(2)}) copy-start(f32[128]{0:T(128)S(1)} %get-tuple-element.395) | copy-start | bytes 1540
  94.4 110.4 %copy-start.25 = (f32[128]{0:T(128)}, f32[128]{0:T(128)S(1)}, u32[]{:S(2)}) copy-start(f32[128]{0:T(128)S(1)} %get-tuple-element.396) | copy-start | bytes 1540
  94.4 110.4 %copy-start.27 = (f32[128]{0:T(128)}, f32[128]{0:T(128)S(1)}, u32[]{:S(2)}) copy-start(f32[128]{0:T(128)S(1)} %get-tuple-element.399) | copy-start | bytes 1540
  94.4 110.4 %copy-start.32 = (f32[128]{0:T(128)}, f32[128]{0:T(128)S(1)}, u32[]{:S(2)}) copy-start(f32[128]{0:T(128)S(1)} %fusion.133) | copy-start | bytes 1540
  94.4 110.4 %copy-start.20 = (f32[3,128]{1,0:T(4,128)S(1)}, f32[3,128]{1,0:T(4,128)}, u32[]{:S(2)}) copy-start(f32[3,128]{1,0:T(4,128)} %param.23) | copy-start | bytes 4612
  94.5 110.4 %copy-start.31 = (f32[3,128]{1,0:T(4,128)S(1)}, f32[3,128]{1,0:T(4,128)}, u32[]{:S(2)}) copy-start(f32[3,128]{1,0:T(4,128)} %param.22) | copy-start | bytes 4612
  97.1 108.5 %copy-start.12 = (f32[3,1,32,128]{3,1,2,0:T(1,128)}, f32[3,1,32,128]{3,1,2,0:T(1,128)S(1)}, u32[]{:S(2)}) copy-start(f32[3,1,32,128]{3,1,2,0:T(1,128)S(1)} %collective-permute-done.1) | copy-start | bytes 147460
  97.8 260.6 %collective-permute-start = (f32[3,1,32,128]{3,1,2,0:T(1,128)}, f32[3,1,32,128]{3,1,2,0:T(1,128)}, u32[]{:S(2)}, u32[]{:S(2)}) collective-permute-start(f32[3,1,32,128]{3,1,2,0:T(1,128)} %get-tuple-element.375), channel_id=1, source_target_pairs={{0,4},{4,8},{8,12},{12,16},{16,20},{20,24},{24,28},{28,0},{1,5},{5... | collective-permute-start | bytes 147464 | tf_op jit(solution)/shard_map/ppermute | solution.py:30
  349.0 9.4 %copy-start.13 = (f32[3,1,32,128]{3,1,2,0:T(1,128)S(1)}, f32[3,1,32,128]{3,1,2,0:T(1,128)}, u32[]{:S(2)}) copy-start(f32[3,1,32,128]{3,1,2,0:T(1,128)} %copy-done.12) | copy-start | bytes 147460
  349.0 16.9 %copy-start.6 = (f32[3,63,32,128]{3,1,2,0:T(8,128)S(1)}, f32[3,63,32,128]{3,1,2,0:T(8,128)}, u32[]{:S(2)}) copy-start(f32[3,63,32,128]{3,1,2,0:T(8,128)} %get-tuple-element.370) | copy-start | bytes 9289732
  358.3 3.0 copy-start.17
  358.3 7.6 %copy-start.5 = (f32[3,64,32,1]{3,1,2,0:T(8,128)S(1)}, f32[3,64,32,1]{3,1,2,0:T(8,128)}, u32[]{:S(2)}) copy-start(f32[3,64,32,1]{3,1,2,0:T(8,128)} %slice.138) | copy-start | bytes 73732
  358.4 7.6 %copy-start.15 = (f32[3,1,32,128]{3,1,2,0:T(1,128)S(1)}, f32[3,1,32,128]{3,1,2,0:T(1,128)}, u32[]{:S(2)}) copy-start(f32[3,1,32,128]{3,1,2,0:T(1,128)} %get-tuple-element.374) | copy-start | bytes 147460
  359.2 4.8 collective-permute-start.2
  359.3 6.6 collective-permute-start.3
  383.7 67.5 %collective-permute-start.5 = (f32[3,1,32,128]{3,2,0,1:T(8,128)S(1)}, f32[3,1,32,128]{3,2,0,1:T(8,128)S(1)}, u32[]{:S(2)}, u32[]{:S(2)}) collective-permute-start(f32[3,1,32,128]{3,2,0,1:T(8,128)S(1)} %bitcast.256), channel_id=1, source_target_pairs={{4,0},{8,4},{12,8},{16,12},{20,16},{24,20},{28,24},{0,28},{5,1},{9... | collective-permute-start | bytes 147464 | tf_op jit(solution)/shard_map/ppermute | solution.py:33
  383.7 67.5 %collective-permute-start.4 = (f32[3,1,32,128]{3,2,0,1:T(8,128)S(1)}, f32[3,1,32,128]{3,2,0,1:T(8,128)S(1)}, u32[]{:S(2)}, u32[]{:S(2)}) collective-permute-start(f32[3,1,32,128]{3,2,0,1:T(8,128)S(1)} %bitcast.251), channel_id=1, source_target_pairs={{0,4},{4,8},{8,12},{12,16},{16,20},{20,24},{24,28},{28,0},{1,5},{5... | collective-permute-start | bytes 147464 | tf_op jit(solution)/shard_map/ppermute | solution.py:30
  389.0 58.6 %copy-start.19 = (s32[6]{0:T(128)S(1)}, s32[6]{0:T(128)}, u32[]{:S(2)}) copy-start(s32[6]{0:T(128)} %copy-done.18) | copy-start | bytes 76
  451.1 119.2 %copy-start.21 = (f32[3,128]{1,0:T(4,128)S(1)}, f32[3,128]{1,0:T(4,128)}, u32[]{:S(2)}) copy-start(f32[3,128]{1,0:T(4,128)} %param.23) | copy-start | bytes 4612
  451.1 119.2 %copy-start.22 = (f32[3,128]{1,0:T(4,128)S(1)}, f32[3,128]{1,0:T(4,128)}, u32[]{:S(2)}) copy-start(f32[3,128]{1,0:T(4,128)} %get-tuple-element.357) | copy-start | bytes 4612
  451.1 119.2 %copy-start.24 = (f32[128]{0:T(128)S(1)}, f32[128]{0:T(128)}, u32[]{:S(2)}) copy-start(f32[128]{0:T(128)} %copy-done.23) | copy-start | bytes 1540
  451.1 119.2 %copy-start.26 = (f32[128]{0:T(128)S(1)}, f32[128]{0:T(128)}, u32[]{:S(2)}) copy-start(f32[128]{0:T(128)} %copy-done.25) | copy-start | bytes 1540
  451.1 119.2 %copy-start.28 = (f32[128]{0:T(128)S(1)}, f32[128]{0:T(128)}, u32[]{:S(2)}) copy-start(f32[128]{0:T(128)} %copy-done.27) | copy-start | bytes 1540
  451.1 119.2 %copy-start.29 = (f32[3]{0:T(128)S(1)}, f32[3]{0:T(128)}, u32[]{:S(2)}) copy-start(f32[3]{0:T(128)} %get-tuple-element.383) | copy-start | bytes 40
  451.1 119.2 %copy-start.30 = (f32[3]{0:T(128)S(1)}, f32[3]{0:T(128)}, u32[]{:S(2)}) copy-start(f32[3]{0:T(128)} %get-tuple-element.384) | copy-start | bytes 40
  451.1 119.2 %copy-start.33 = (f32[128]{0:T(128)S(1)}, f32[128]{0:T(128)}, u32[]{:S(2)}) copy-start(f32[128]{0:T(128)} %copy-done.32) | copy-start | bytes 1540
  451.2 119.9 %copy-start.8 = (f32[3,1,32,128]{3,2,0,1:T(8,128)}, f32[3,1,32,128]{3,2,0,1:T(8,128)S(1)}, u32[]{:S(2)}) copy-start(f32[3,1,32,128]{3,2,0,1:T(8,128)S(1)} %collective-permute-done.5) | copy-start | bytes 147460
  451.2 119.9 %copy-start.10 = (f32[3,1,32,128]{3,2,0,1:T(8,128)}, f32[3,1,32,128]{3,2,0,1:T(8,128)S(1)}, u32[]{:S(2)}) copy-start(f32[3,1,32,128]{3,2,0,1:T(8,128)S(1)} %collective-permute-done.4) | copy-start | bytes 147460
  451.9 268.3 %collective-permute-start.6 = (f32[3,66,1,128]{3,1,2,0:T(8,128)}, f32[3,66,1,128]{3,1,2,0:T(8,128)}, u32[]{:S(2)}, u32[]{:S(2)}) collective-permute-start(f32[3,66,1,128]{3,1,2,0:T(8,128)} %get-tuple-element.360), channel_id=1, source_target_pairs={{1,0},{2,1},{3,2},{0,3},{5,4},{6,5},{7,6},{4,7},{9,8},{10,9},{11,1... | collective-permute-start | bytes 304136 | tf_op jit(solution)/shard_map/ppermute | solution.py:33
  451.9 268.4 %collective-permute-start.7 = (f32[3,66,1,128]{3,1,2,0:T(8,128)}, f32[3,66,1,128]{3,1,2,0:T(8,128)}, u32[]{:S(2)}, u32[]{:S(2)}) collective-permute-start(f32[3,66,1,128]{3,1,2,0:T(8,128)} %get-tuple-element.361), channel_id=1, source_target_pairs={{0,1},{1,2},{2,3},{3,0},{4,5},{5,6},{6,7},{7,4},{8,9},{9,10},{10,1... | collective-permute-start | bytes 304136 | tf_op jit(solution)/shard_map/ppermute | solution.py:30
  710.9 9.4 %copy-start.4 = (f32[3,64,32,1]{3,1,2,0:T(8,128)S(1)}, f32[3,64,32,1]{3,1,2,0:T(8,128)}, u32[]{:S(2)}) copy-start(f32[3,64,32,1]{3,1,2,0:T(8,128)} %slice.149) | copy-start | bytes 73732
  710.9 9.4 %copy-start.9 = (f32[3,1,32,128]{3,2,0,1:T(8,128)S(1)}, f32[3,1,32,128]{3,2,0,1:T(8,128)}, u32[]{:S(2)}) copy-start(f32[3,1,32,128]{3,2,0,1:T(8,128)} %copy-done.8) | copy-start | bytes 147460
  710.9 9.4 %copy-start.11 = (f32[3,1,32,128]{3,2,0,1:T(8,128)S(1)}, f32[3,1,32,128]{3,2,0,1:T(8,128)}, u32[]{:S(2)}) copy-start(f32[3,1,32,128]{3,2,0,1:T(8,128)} %copy-done.10) | copy-start | bytes 147460
  711.0 9.4 %copy-start.14 = (f32[3,1,32,128]{3,2,0,1:T(8,128)S(1)}, f32[3,1,32,128]{3,2,0,1:T(8,128)}, u32[]{:S(2)}) copy-start(f32[3,1,32,128]{3,2,0,1:T(8,128)} %broadcast_select_fusion.1) | copy-start | bytes 147460
  711.0 9.4 %copy-start.16 = (f32[3,32,128]{2,1,0:T(8,128)S(1)}, f32[3,32,128]{2,1,0:T(8,128)}, u32[]{:S(2)}) copy-start(f32[3,32,128]{2,1,0:T(8,128)} %bitcast_select_fusion) | copy-start | bytes 147460
  720.3 10.1 %copy-start.1 = (s32[32,2]{0,1:T(2,128)S(1)}, s32[32,2]{0,1:T(2,128)}, u32[]{:S(2)}) copy-start(s32[32,2]{0,1:T(2,128)} %param.20) | copy-start | bytes 772
Sparse Core Ops, SparseCore 0:
  81.0 122.9 all-reduce.10
  451.3 118.2 all-reduce.12
where the time goes:
time: 742 us; the launch traced here: 737 us
  waiting for transfers between devices  225 us (30%)
  local copies, waits for them, and re-layouts  179 us (24%)
  blocking collectives  139 us (19%)
  loops' own time  104 us (14%)
  other arithmetic  39.6 us (5%)
  matrix products  31.7 us (4%)
  between operations  14.7 us (2%)
    unnamed x4, waiting for transfers between devices  220 us
    all_gather x2, blocking collectives, per_device(): lax.all_gather(own_forces.reshape(own_count, components * sections), ('gx...  139 us
    another operation x2, loops' own time, per_device(): lax.fori_loop(0, live_slots, sample_slot, jnp.zeros((list_len, components...  54.6 us
    another operation x2, loops' own time, per_device(): lax.fori_loop(0, live_slots, spread_slot, jnp.zeros_like(padded))  49.5 us
    dynamic_slice x24, local copies, waits for them, and re-layouts, spread_slot(): corner = (0, start_x[slot_id], start_y[slot_id], 0)  29.1 us
    dynamic_update_slice x12, local copies, waits for them, and re-layouts, spread_slot(): return lax.dynamic_update_slice(force_field, current + block_add, corner)  22.7 us
    while x2, local copies, waits for them, and re-layouts, per_device(): lax.fori_loop(0, live_slots, spread_slot, jnp.zeros_like(padded))  18.6 us
    dynamic_slice x12, local copies, waits for them, and re-layouts, sample_slot(): start_x[slot_id]  15.5 us
  transfers between devices with their start and end apart: 10, of which 4 were waited for; matrix products, arithmetic and copies ran while one was open for 24% of the time, Pallas kernels for 0%

commit v1 on v0

v1 whole, which is shorter than its diff:
```python
import functools
import math

import jax
import jax.numpy as jnp
from jax import lax
from jax.experimental import pallas as pl
from jax.experimental.pallas import tpu as pltpu
from jax.sharding import PartitionSpec as P

RADIUS = 12
HUB = 15
STEPS = 2
EPSILON = 2.0
SUPPORT = 3.0
TURN_RATE = 0.1
SPIN = 0.25
LIFT_SLOPE = 2.0 * math.pi
FORCE_SCALE = 0.15
ADVECT = 0.5
DIFFUSE = 0.05
PRECISE = lax.Precision.HIGHEST
MESH = pl.DeviceIdType.MESH
BLADES = 3
ENTRIES = 2
ROWS = 8
CHUNKS = 4


def taper_const(distance):
    square = distance * distance
    term = max(1.0 - square / (SUPPORT * SUPPORT), 0.0)
    return math.exp(-square / EPSILON**2) * term * term / (EPSILON * math.sqrt(math.pi))


KERN_X = [taper_const(float(i)) for i in range(3)]


def taper_kernel(distance):
    square = distance * distance
    term = jnp.maximum(1.0 - square * (1.0 / (SUPPORT * SUPPORT)), 0.0)
    return (
        jnp.exp(square * (-1.0 / (EPSILON * EPSILON)))
        * (term * term)
        * (1.0 / (EPSILON * math.sqrt(math.pi)))
    )


def weight_x(offset):
    dist = jnp.abs(offset)
    return jnp.where(
        dist == 0,
        KERN_X[0],
        jnp.where(dist == 1, KERN_X[1], jnp.where(dist == 2, KERN_X[2], 0.0)),
    ).astype(jnp.float32)


def farm_kernel(
    nx,
    ny,
    vel_hbm,
    inflow_ref,
    az_ref,
    pos_ref,
    cross_ref,
    lag_ref,
    rate_ref,
    chord_ref,
    twist_ref,
    out_hbm,
    state_ref,
    grid0,
    grid1,
    grid2,
    halo_x,
    halo_y,
    face_y,
    part_out,
    part_in,
    kern_y,
    kern_z,
    spread,
    lag_pack,
    lag_g1,
    lag_g2,
    end_pack,
    end_g1,
    end_g2,
    load_sem,
    store_sem,
    hx_send,
    hx_recv,
    hy_send,
    hy_recv,
    ps_send,
    ps_recv,
    gy_send,
    gy_recv,
    gx_send,
    gx_recv,
):
    grids = (grid0, grid1, grid2)
    _, cx2, cy, nz = grid0.shape
    cx = cx2 - 2
    total_y = cy * ny
    gx = lax.axis_index("gx")
    gy = lax.axis_index("gy")
    tile = gx * ny + gy
    east = lax.rem(gx + 1, nx)
    west = lax.rem(gx + nx - 1, nx)
    up = lax.rem(gy + 1, ny)
    down = lax.rem(gy + ny - 1, ny)

    load = pltpu.make_async_copy(vel_hbm, grid0.at[:, pl.ds(1, cx)], load_sem)
    load.start()

    barrier = pltpu.get_barrier_semaphore()
    for d in range(1, ny):
        pl.semaphore_signal(
            barrier, inc=1, device_id={"gy": lax.rem(gy + d, ny)}, device_id_type=MESH
        )
    for d in range(1, nx):
        pl.semaphore_signal(
            barrier, inc=1, device_id={"gx": lax.rem(gx + d, nx)}, device_id_type=MESH
        )

    rotor, hub_x, load_x, shift_y, valid, az = [], [], [], [], [], []
    for e in range(ENTRIES):
        blade = cross_ref[BLADES * e, tile]
        r = jnp.where(blade >= 0, blade, 0) // BLADES
        rotor.append(jnp.where(blade >= 0, r, -1))
        valid.append(jnp.where(blade >= 0, 1.0, 0.0).astype(jnp.float32))
        hub_x.append(jnp.where(blade >= 0, pos_ref[0, r] - gx * cx, 2))
        load_x.append(jnp.clip(hub_x[e], 2, cx - 3))
        off = gy * cy - pos_ref[1, r] + total_y + total_y // 2
        shift_y.append(lax.rem(off, total_y) - total_y // 2)
        az.append(az_ref[r])

    def matches(other):
        found = []
        for f in range(ENTRIES):
            blade = cross_ref[BLADES * f, other]
            found.append(jnp.where(blade >= 0, jnp.where(blade >= 0, blade, 0) // BLADES, -2))
        return [
            [jnp.where(rotor[e] == found[f], 1.0, 0.0).astype(jnp.float32) for f in range(ENTRIES)]
            for e in range(ENTRIES)
        ]

    row = lax.broadcasted_iota(jnp.int32, (ROWS, nz), 0)
    first = row < BLADES
    lane8 = lax.broadcasted_iota(jnp.int32, (ROWS, nz), 1).astype(jnp.float32)
    radius = RADIUS * (lane8 + 0.5) / nz
    spin = jnp.where(first, row, row - BLADES).astype(jnp.float32) * (2.0 * math.pi / 3.0)
    base = jnp.where(first, az[0], az[1])
    mask_rows = []
    for other in (gx * ny + down, gx * ny + up):
        m = matches(other)
        mask_rows.append(
            (jnp.where(first, m[0][0], m[1][1]), jnp.where(first, m[0][1], m[1][0]))
        )
    cos_all, sin_all = [], []
    rows_y = lax.broadcasted_iota(jnp.int32, (cy, nz), 0)
    rows_z = lax.broadcasted_iota(jnp.int32, (nz, nz), 0).astype(jnp.float32) - HUB
    for n in range(STEPS):
        theta = base + TURN_RATE * n + spin
        cos_n, sin_n = jnp.cos(theta), jnp.sin(theta)
        cos_all.append(cos_n)
        sin_all.append(sin_n)
        rc, rs = radius * cos_n, radius * sin_n
        for e in range(ENTRIES):
            y_rel = (rows_y + shift_y[e]).astype(jnp.float32)
            for b in range(BLADES):
                i = BLADES * e + b
                kern_y[n, e, :, b * nz : (b + 1) * nz] = taper_kernel(y_rel - rs[i : i + 1]) * valid[e]
                kern_z[n, e, :, b * nz : (b + 1) * nz] = taper_kernel(rows_z - rc[i : i + 1])
    cos_t, sin_t = jnp.cos(twist_ref[...]), jnp.sin(twist_ref[...])
    chord = FORCE_SCALE * chord_ref[...]

    lag_pack[0:BLADES] = lag_ref[...]
    lag_pack[BLADES : 2 * BLADES] = rate_ref[...]
    lag_pack[2 * BLADES : ROWS] = jnp.zeros((ROWS - 2 * BLADES, nz), jnp.float32)

    pl.semaphore_wait(barrier, nx - 1 + ny - 1)

    started = []

    def send(src, dst, send_sem, recv_sem, axis, peer):
        copy = pltpu.make_async_remote_copy(
            src_ref=src,
            dst_ref=dst,
            send_sem=send_sem,
            recv_sem=recv_sem,
            device_id={axis: peer},
            device_id_type=MESH,
        )
        copy.start()
        started.append(copy)
        return copy

    def gather_start(k, pack, first_level):
        copies = [
            send(pack, first_level.at[gy], gy_send.at[k, d], gy_recv.at[k, d], "gy", lax.rem(gy + d, ny))
            for d in range(1, ny)
        ]
        first_level[gy] = pack[...]
        return copies

    def gather_next(k, copies, first_level, second_level):
        for copy in copies:
            copy.wait_recv()
        copies = [
            send(first_level, second_level.at[gx], gx_send.at[k, d], gx_recv.at[k, d], "gx", lax.rem(gx + d, nx))
            for d in range(1, nx)
        ]
        second_level[gx] = first_level[...]
        return copies

    lag_copies = gather_start(0, lag_pack, lag_g1)
    load.wait()

    lag = None
    rate = None
    zero_rows = jnp.zeros((ROWS - 2 * BLADES, nz), jnp.float32)
    lane = lax.broadcasted_iota(jnp.int32, (cy, nz), 1)
    row_c = lax.broadcasted_iota(jnp.int32, (cy, nz), 0)
    is_first_z, is_last_z = lane == 0, lane == nz - 1
    is_first_y, is_last_y = row_c == 0, row_c == cy - 1
    end_copies = None
    stores = []
    for n in range(STEPS):
        src, dst = grids[n], grids[n + 1]
        halo_copies = [
            send(src.at[:, cx], halo_x.at[n, 0], hx_send.at[n, 0], hx_recv.at[n, 0], "gx", east),
            send(src.at[:, 1], halo_x.at[n, 1], hx_send.at[n, 1], hx_recv.at[n, 1], "gx", west),
        ]
        flat = src.reshape(3 * cx2 * cy, nz)
        for c in range(3):
            start = (c * cx2 + 1) * cy
            face_y[n, 0, c] = flat[pl.ds(start + cy - 1, cx, stride=cy), :]
            face_y[n, 1, c] = flat[pl.ds(start, cx, stride=cy), :]
        halo_copies += [
            send(face_y.at[n, 0], halo_y.at[n, 0], hy_send.at[n, 0], hy_recv.at[n, 0], "gy", up),
            send(face_y.at[n, 1], halo_y.at[n, 1], hy_send.at[n, 1], hy_recv.at[n, 1], "gy", down),
        ]

        sampled = [[], [], []]
        for e in range(ENTRIES):
            field = None
            for i in range(-2, 3):
                term = KERN_X[abs(i)] * src[:, load_x[e] + 1 + i]
                field = term if field is None else field + term
            inner = jnp.dot(
                field.reshape(3 * cy, nz),
                kern_z[n, e],
                precision=PRECISE,
                preferred_element_type=jnp.float32,
            )
            for c in range(3):
                reduced = jnp.sum(inner[c * cy : (c + 1) * cy] * kern_y[n, e], axis=0, keepdims=True)
                sampled[c] += [reduced[:, b * nz : (b + 1) * nz] for b in range(BLADES)]
        for c in range(3):
            part_out[n, c] = jnp.concatenate(sampled[c] + [zero_rows], axis=0)
        part_copies = [
            send(part_out.at[n], part_in.at[n, 0], ps_send.at[n, 0], ps_recv.at[n, 0], "gy", up),
            send(part_out.at[n], part_in.at[n, 1], ps_send.at[n, 1], ps_recv.at[n, 1], "gy", down),
        ]
        if n == 0:
            lag_copies = gather_next(0, lag_copies, lag_g1, lag_g2)

        for copy in halo_copies:
            copy.wait_recv()
        src[:, 0] = jnp.where(gx == 0, inflow_ref[...], halo_x[n, 0])
        src[:, cx + 1] = jnp.where(gx == nx - 1, src[:, cx], halo_x[n, 1])

        def plane(x, carry):
            for c in range(3):
                cur = src[c, x + 1]
                y_prev = jnp.where(is_first_y, halo_y[n, 0, c, pl.ds(x, 1), :], pltpu.roll(cur, 1, 0))
                y_next = jnp.where(is_last_y, halo_y[n, 1, c, pl.ds(x, 1), :], pltpu.roll(cur, cy - 1, 0))
                z_prev = jnp.where(is_first_z, 0.0, pltpu.roll(cur, 1, 1))
                z_next = jnp.where(is_last_z, cur, pltpu.roll(cur, nz - 1, 1))
                others = src[c, x + 2] + y_prev + y_next + z_prev + z_next
                dst[c, x + 1] = (
                    (1.0 - ADVECT - 6.0 * DIFFUSE) * cur
                    + (ADVECT + DIFFUSE) * src[c, x]
                    + DIFFUSE * others
                )
            return carry

        lax.fori_loop(0, cx, plane, 0)

        for copy in part_copies:
            copy.wait_recv()
        whole = []
        for c in range(3):
            total = part_out[n, c]
            for side in range(2):
                other = part_in[n, side, c]
                same, cross = mask_rows[side]
                swapped = jnp.where(first, pltpu.roll(other, ROWS - BLADES, 0), pltpu.roll(other, BLADES, 0))
                total = total + (same * other + cross * swapped)
            whole.append(total)
        if n == 0:
            for copy in lag_copies:
                copy.wait_recv()
            state_rows, rate_rows = [], []
            for e in range(ENTRIES):
                r = jnp.maximum(rotor[e], 0)
                block = lag_g2[r // ny, lax.rem(r, ny)]
                state_rows.append(block[0:BLADES])
                rate_rows.append(block[BLADES : 2 * BLADES])
            lag = jnp.concatenate(state_rows + [zero_rows], axis=0)
            rate = jnp.concatenate(rate_rows + [zero_rows], axis=0)
        cos_b, sin_b = cos_all[n], sin_all[n]
        axial = whole[0]
        tangential = SPIN * radius - (whole[1] * cos_b - whole[2] * sin_b)
        magnitude = jnp.sqrt(axial * axial + tangential * tangential + 1.0)
        lift_static = LIFT_SLOPE * (axial * cos_t - tangential * sin_t) / magnitude
        lag = lag + rate * (lift_static - lag)
        if n == STEPS - 1:
            end_pack[...] = lag
            end_copies = gather_start(1, end_pack, end_g1)
        lift = chord * lag * magnitude
        forces = (-lift * tangential, lift * axial * cos_b, -lift * axial * sin_b)
        for e in range(ENTRIES):
            weighted = []
            for c in range(3):
                weighted.append(
                    jnp.concatenate(
                        [
                            forces[c][BLADES * e + b : BLADES * e + b + 1]
                            * kern_y[n, e, :, b * nz : (b + 1) * nz]
                            for b in range(BLADES)
                        ],
                        axis=1,
                    )
                )
            pushed = lax.dot_general(
                jnp.concatenate(weighted, axis=0),
                kern_z[n, e],
                (((1,), (1,)), ((), ())),
                precision=PRECISE,
                preferred_element_type=jnp.float32,
            )
            spread[n, e] = pushed.reshape(3, cy, nz)
        if n == STEPS - 1:
            end_copies = gather_next(1, end_copies, end_g1, end_g2)

        def push(x, carry):
            w0, w1 = weight_x(x - hub_x[0]), weight_x(x - hub_x[1])
            for c in range(3):
                dst[c, x + 1] = dst[c, x + 1] + (w0 * spread[n, 0, c] + w1 * spread[n, 1, c])
            return carry

        if n < STEPS - 1:
            lax.fori_loop(0, cx, push, 0)
        else:
            size = cx // CHUNKS
            for k in range(CHUNKS):
                lax.fori_loop(k * size, (k + 1) * size, push, 0)
                store = pltpu.make_async_copy(
                    dst.at[:, pl.ds(1 + k * size, size)],
                    out_hbm.at[:, pl.ds(k * size, size)],
                    store_sem.at[k],
                )
                store.start()
                stores.append(store)

    for copy in end_copies:
        copy.wait_recv()
    home_x = pos_ref[0, tile] // cx
    home_y = pos_ref[1, tile] // cy
    block = end_g2[home_x, home_y]
    in_first = cross_ref[0, home_x * ny + home_y] == BLADES * tile
    state_ref[...] = jnp.where(in_first, block[0:BLADES], block[BLADES : 2 * BLADES])
    for copy in started:
        copy.wait_send()
    for store in stores:
        store.wait()


def per_device(
    velocity, inflow, azimuth, positions, crossings, lag_state, lag_rate, chord_len, twist_angle
):
    nx = lax.axis_size("gx")
    ny = lax.axis_size("gy")
    comps, cx, cy, nz = velocity.shape
    own, sections = lag_state.shape
    assert comps == 3 and own == BLADES and sections == nz
    f32 = jnp.float32
    grid = pltpu.VMEM((3, cx + 2, cy, nz), f32)
    dma = pltpu.SemaphoreType.DMA
    vmem = pl.BlockSpec(memory_space=pltpu.VMEM)
    smem = pl.BlockSpec(memory_space=pltpu.SMEM)
    hbm = pl.BlockSpec(memory_space=pl.ANY)
    return pl.pallas_call(
        functools.partial(farm_kernel, nx, ny),
        out_shape=(
            jax.ShapeDtypeStruct(velocity.shape, f32),
            jax.ShapeDtypeStruct(lag_state.shape, f32),
        ),
        in_specs=[hbm, vmem, smem, smem, smem, vmem, vmem, vmem, vmem],
        out_specs=(hbm, vmem),
        scratch_shapes=[
            grid,
            grid,
            grid,
            pltpu.VMEM((STEPS, 2, 3, cy, nz), f32),
            pltpu.VMEM((STEPS, 2, 3, cx, nz), f32),
            pltpu.VMEM((STEPS, 2, 3, cx, nz), f32),
            pltpu.VMEM((STEPS, 3, ROWS, nz), f32),
            pltpu.VMEM((STEPS, 2, 3, ROWS, nz), f32),
            pltpu.VMEM((STEPS, ENTRIES, cy, BLADES * nz), f32),
            pltpu.VMEM((STEPS, ENTRIES, nz, BLADES * nz), f32),
            pltpu.VMEM((STEPS, ENTRIES, 3, cy, nz), f32),
            pltpu.VMEM((ROWS, nz), f32),
            pltpu.VMEM((ny, ROWS, nz), f32),
            pltpu.VMEM((nx, ny, ROWS, nz), f32),
            pltpu.VMEM((ROWS, nz), f32),
            pltpu.VMEM((ny, ROWS, nz), f32),
            pltpu.VMEM((nx, ny, ROWS, nz), f32),
            dma,
            dma((CHUNKS,)),
            dma((STEPS, 2)),
            dma((STEPS, 2)),
            dma((STEPS, 2)),
            dma((STEPS, 2)),
            dma((STEPS, 2)),
            dma((STEPS, 2)),
            dma((2, ny)),
            dma((2, ny)),
            dma((2, nx)),
            dma((2, nx)),
        ],
        compiler_params=pltpu.CompilerParams(
            collective_id=0, has_side_effects=True, vmem_limit_bytes=60 * 1024 * 1024
        ),
        cost_estimate=pl.CostEstimate(
            flops=50_000_000, bytes_accessed=8 * velocity.size, transcendentals=500_000
        ),
    )(
        velocity,
        inflow,
        azimuth,
        positions.T,
        crossings.T,
        lag_state,
        lag_rate,
        chord_len.reshape(1, sections),
        twist_angle.reshape(1, sections),
    )


def solution(mesh):
    return jax.shard_map(
        per_device,
        mesh=mesh,
        in_specs=(
            P(None, "gx", "gy", None),
            P(None, "gy", None),
            P(),
            P(),
            P(),
            P(("gx", "gy"), None),
            P(("gx", "gy"), None),
            P(),
            P(),
        ),
        out_specs=(P(None, "gx", "gy", None), P(("gx", "gy"), None)),
        check_vma=False,
    )
```

time: 742 us -> 46.7 us (0.06)
  waiting for transfers between devices: 225 us -> 0 us
  local copies, waits for them, and re-layouts: 179 us -> 4.44 us
  blocking collectives: 139 us -> 0 us
  loops' own time: 104 us -> 0 us
  Pallas kernels: 0 us -> 41.4 us
  other arithmetic: 39.6 us -> 0 us
  matrix products: 31.7 us -> 0 us
  between operations: 14.7 us -> 0.65 us
    unnamed x4 -> x0, waiting for transfers between devices: 220 us -> none
    all_gather x2 -> x0, blocking collectives: 139 us -> none  [per_device(): lax.all_gather(own_forces.reshape(own_count, components * sections), ('gx...]
    another operation x4 -> x0, loops' own time: 104 us -> none  [the longest x2 54.6 us: per_device(): lax.fori_loop(0, live_slots, sample_slot, jnp.zeros((list_len, components...]
    dynamic_slice x60 -> x0, local copies, waits for them, and re-layouts: 70.8 us -> none  [the longest x24 29.1 us: spread_slot(): corner = (0, start_x[slot_id], start_y[slot_id], 0)]
    pallas_call x0 -> x1, Pallas kernels: none -> 41.4 us  [per_device(): pl.pallas_call(functools.partial(farm_kernel, nx, ny), out_shape=(jax.Sha...]
    dot_general x40 -> x0, matrix products: 31.7 us -> none  [the longest x12 12.4 us: spread_slot(): jnp.dot(weighted.reshape(-1, sections), kern_z[slot_id], precision=PRECISE)]
    add x14 -> x0, other arithmetic: 28 us -> none  [the longest x2 15.1 us: advance_tile(): velocity + ADVECT * (x_prev - velocity)]
    dynamic_update_slice x24 -> x0, local copies, waits for them, and re-layouts: 22.8 us -> none  [the longest x12 22.7 us: spread_slot(): return lax.dynamic_update_slice(force_field, current + block_add, corner)]
  transfers between devices with their start and end apart: 10 -> 0, of which waited for: 4 -> 0; matrix products, arithmetic and copies ran while one was open for 24% -> 0% of each run, Pallas kernels for 0% -> 0%
where the time goes in v1:
time: 46.7 us; the launch traced here: 46.5 us
  Pallas kernels  41.4 us (89%)
  local copies, waits for them, and re-layouts  4.44 us (10%)
  between operations  0.65 us (1%)
    pallas_call x1, Pallas kernels, per_device(): pl.pallas_call(functools.partial(farm_kernel, nx, ny), out_shape=(jax.Sha...  41.4 us
    unnamed x4, local copies, waits for them, and re-layouts  4.44 us

profile of v1, /device:TPU:0, one launch (start us, length us, event | category | flops | bytes accessed | tf_op | source)
XLA Modules:
  0.0 46.5 jit_solution(15288577514901323062)
XLA Ops:
  0.6 41.4 %shard_map.104 = (f32[3,64,32,128]{3,2,1,0:T(8,128)}, f32[3,128]{1,0:T(4,128)}) custom-call(f32[3,64,32,128]{3,2,1,0:T(8,128)} %vel_hbm.1, f32[3,32,128]{2,1,0:T(8,128)} %inflow_ref.1, f32[32]{0:T(128)} %az_ref.1, s32[2,32]{1,0:T(2,128)} %bitcast.5, s32[6,32]{1,0:T(8,128)} %bitcast.4, f32[3,128]{1,0:T(4,128)} %lag_ref.1, f32[3,128]{1,0:T(4,128)} %rate_ref.1, ...), custom_call_target="tpu_custom_call" | custom-call | flops 50000000 | bytes 6291456 | tf_op jit(solution)/shard_map/pallas_call | solution.py:396
  42.0 0.0 copy-start
  42.0 3.9 %copy.13 = f32[3,64,32,128]{3,2,1,0:T(8,128)} copy(f32[3,64,32,128]{3,2,1,0:T(8,128)} %get-tuple-element.4) | data formatting | bytes 6291456
  45.9 0.0 copy-done
  45.9 0.6 %copy.14 = f32[3,128]{1,0:T(4,128)} copy(f32[3,128]{1,0:T(4,128)S(1)} %copy-done) | data formatting | bytes 3072
Async XLA Ops:
  42.0 3.9 %copy-start = (f32[3,128]{1,0:T(4,128)S(1)}, f32[3,128]{1,0:T(4,128)}, u32[]{:S(2)}) copy-start(f32[3,128]{1,0:T(4,128)} %get-tuple-element.5) | copy-start | bytes 4612

commit v2 on v1

--- a/solution.py
+++ b/solution.py
@@ -24,7 +24,8 @@
 BLADES = 3
 ENTRIES = 2
 ROWS = 8
-CHUNKS = 4
+CHUNKS = 3
+UNROLL = 4
 
 
 def taper_const(distance):
@@ -102,6 +103,7 @@
     grids = (grid0, grid1, grid2)
     _, cx2, cy, nz = grid0.shape
     cx = cx2 - 2
+    split = cx // 2
     total_y = cy * ny
     gx = lax.axis_index("gx")
     gy = lax.axis_index("gy")
@@ -233,15 +235,6 @@
             send(src.at[:, cx], halo_x.at[n, 0], hx_send.at[n, 0], hx_recv.at[n, 0], "gx", east),
             send(src.at[:, 1], halo_x.at[n, 1], hx_send.at[n, 1], hx_recv.at[n, 1], "gx", west),
         ]
-        flat = src.reshape(3 * cx2 * cy, nz)
-        for c in range(3):
-            start = (c * cx2 + 1) * cy
-            face_y[n, 0, c] = flat[pl.ds(start + cy - 1, cx, stride=cy), :]
-            face_y[n, 1, c] = flat[pl.ds(start, cx, stride=cy), :]
-        halo_copies += [
-            send(face_y.at[n, 0], halo_y.at[n, 0], hy_send.at[n, 0], hy_recv.at[n, 0], "gy", up),
-            send(face_y.at[n, 1], halo_y.at[n, 1], hy_send.at[n, 1], hy_recv.at[n, 1], "gy", down),
-        ]
 
         sampled = [[], [], []]
         for e in range(ENTRIES):
@@ -264,30 +257,40 @@
             send(part_out.at[n], part_in.at[n, 0], ps_send.at[n, 0], ps_recv.at[n, 0], "gy", up),
             send(part_out.at[n], part_in.at[n, 1], ps_send.at[n, 1], ps_recv.at[n, 1], "gy", down),
         ]
+        flat = src.reshape(3 * cx2 * cy, nz)
+        for c in range(3):
+            start = (c * cx2 + 1) * cy
+            face_y[n, 0, c] = flat[pl.ds(start + cy - 1, cx, stride=cy), :]
+            face_y[n, 1, c] = flat[pl.ds(start, cx, stride=cy), :]
+        halo_copies += [
+            send(face_y.at[n, 0], halo_y.at[n, 0], hy_send.at[n, 0], hy_recv.at[n, 0], "gy", up),
+            send(face_y.at[n, 1], halo_y.at[n, 1], hy_send.at[n, 1], hy_recv.at[n, 1], "gy", down),
+        ]
         if n == 0:
             lag_copies = gather_next(0, lag_copies, lag_g1, lag_g2)
 
-        for copy in halo_copies:
-            copy.wait_recv()
-        src[:, 0] = jnp.where(gx == 0, inflow_ref[...], halo_x[n, 0])
-        src[:, cx + 1] = jnp.where(gx == nx - 1, src[:, cx], halo_x[n, 1])
-
-        def plane(x, carry):
+        def halo_rows(c, x):
+            return halo_y[n, 0, c, pl.ds(x, 1), :], halo_y[n, 1, c, pl.ds(x, 1), :]
+
+        def moved(c, x, below, above):
+            cur = src[c, x + 1]
+            y_prev = jnp.where(is_first_y, below, pltpu.roll(cur, 1, 0))
+            y_next = jnp.where(is_last_y, above, pltpu.roll(cur, cy - 1, 0))
+            z_prev = jnp.where(is_first_z, 0.0, pltpu.roll(cur, 1, 1))
+            z_next = jnp.where(is_last_z, cur, pltpu.roll(cur, nz - 1, 1))
+            others = (src[c, x + 2] + (y_prev + y_next)) + (z_prev + z_next)
+            return (
+                (1.0 - ADVECT - 6.0 * DIFFUSE) * cur
+                + (ADVECT + DIFFUSE) * src[c, x]
+                + DIFFUSE * others
+            )
+
+        def plane_alone(x, carry):
             for c in range(3):
-                cur = src[c, x + 1]
-                y_prev = jnp.where(is_first_y, halo_y[n, 0, c, pl.ds(x, 1), :], pltpu.roll(cur, 1, 0))
-                y_next = jnp.where(is_last_y, halo_y[n, 1, c, pl.ds(x, 1), :], pltpu.roll(cur, cy - 1, 0))
-                z_prev = jnp.where(is_first_z, 0.0, pltpu.roll(cur, 1, 1))
-                z_next = jnp.where(is_last_z, cur, pltpu.roll(cur, nz - 1, 1))
-                others = src[c, x + 2] + y_prev + y_next + z_prev + z_next
-                dst[c, x + 1] = (
-                    (1.0 - ADVECT - 6.0 * DIFFUSE) * cur
-                    + (ADVECT + DIFFUSE) * src[c, x]
-                    + DIFFUSE * others
-                )
+                dst[c, x + 1] = moved(c, x, 0.0, 0.0)
             return carry
 
-        lax.fori_loop(0, cx, plane, 0)
+        lax.fori_loop(1, split, plane_alone, 0, unroll=UNROLL)
 
         for copy in part_copies:
             copy.wait_recv()
@@ -343,28 +346,49 @@
                 preferred_element_type=jnp.float32,
             )
             spread[n, e] = pushed.reshape(3, cy, nz)
+        for copy in halo_copies:
+            copy.wait_recv()
+        src[:, 0] = jnp.where(gx == 0, inflow_ref[...], halo_x[n, 0])
+        src[:, cx + 1] = jnp.where(gx == nx - 1, src[:, cx], halo_x[n, 1])
+
+        def body_force(c, x):
+            w0, w1 = weight_x(x - hub_x[0]), weight_x(x - hub_x[1])
+            return w0 * spread[n, 0, c] + w1 * spread[n, 1, c]
+
+        def plane_whole(x, carry):
+            for c in range(3):
+                below, above = halo_rows(c, x)
+                dst[c, x + 1] = moved(c, x, below, above) + body_force(c, x)
+            return carry
+
+        def plane_rest(x, carry):
+            for c in range(3):
+                below, above = halo_rows(c, x)
+                edge = jnp.where(is_first_y, below, jnp.where(is_last_y, above, 0.0))
+                dst[c, x + 1] = dst[c, x + 1] + (body_force(c, x) + DIFFUSE * edge)
+            return carry
+
+        def store(k, low, high):
+            if n == STEPS - 1:
+                copy = pltpu.make_async_copy(
+                    dst.at[:, pl.ds(1 + low, high - low)],
+                    out_hbm.at[:, pl.ds(low, high - low)],
+                    store_sem.at[k],
+                )
+                copy.start()
+                stores.append(copy)
+
+        lax.fori_loop(split, cx - 1, plane_whole, 0, unroll=UNROLL)
         if n == STEPS - 1:
             end_copies = gather_next(1, end_copies, end_g1, end_g2)
-
-        def push(x, carry):
-            w0, w1 = weight_x(x - hub_x[0]), weight_x(x - hub_x[1])
-            for c in range(3):
-                dst[c, x + 1] = dst[c, x + 1] + (w0 * spread[n, 0, c] + w1 * spread[n, 1, c])
-            return carry
-
-        if n < STEPS - 1:
-            lax.fori_loop(0, cx, push, 0)
-        else:
-            size = cx // CHUNKS
-            for k in range(CHUNKS):
-                lax.fori_loop(k * size, (k + 1) * size, push, 0)
-                store = pltpu.make_async_copy(
-                    dst.at[:, pl.ds(1 + k * size, size)],
-                    out_hbm.at[:, pl.ds(k * size, size)],
-                    store_sem.at[k],
-                )
-                store.start()
-                stores.append(store)
+        plane_whole(cx - 1, 0)
+        store(0, split, cx)
+        plane_whole(0, 0)
+        half = split // 2
+        lax.fori_loop(1, half, plane_rest, 0, unroll=UNROLL)
+        store(1, 0, half)
+        lax.fori_loop(half, split, plane_rest, 0, unroll=UNROLL)
+        store(2, half, split)
 
     for copy in end_copies:
         copy.wait_recv()
@@ -375,8 +399,8 @@
     state_ref[...] = jnp.where(in_first, block[0:BLADES], block[BLADES : 2 * BLADES])
     for copy in started:
         copy.wait_send()
-    for store in stores:
-        store.wait()
+    for copy in stores:
+        copy.wait()
 
 
 def per_device(

time: 46.7 us -> 34.6 us (0.74)
  Pallas kernels: 41.4 us -> 29.3 us
    pallas_call x1, Pallas kernels: 41.4 us -> 29.3 us  [per_device(): pl.pallas_call(functools.partial(farm_kernel, nx, ny), out_shape=(jax.Sha...]
where the time goes in v2:
time: 34.6 us; the launch traced here: 34.4 us
  Pallas kernels  29.3 us (85%)
  local copies, waits for them, and re-layouts  4.44 us (13%)
  between operations  0.65 us (2%)
    pallas_call x1, Pallas kernels, per_device(): pl.pallas_call(functools.partial(farm_kernel, nx, ny), out_shape=(jax.Sha...  29.3 us
    unnamed x4, local copies, waits for them, and re-layouts  4.44 us

profile of v2, /device:TPU:0, one launch (start us, length us, event | category | flops | bytes accessed | tf_op | source)
XLA Modules:
  0.0 34.4 jit_solution(17501202156054429378)
XLA Ops:
  0.6 29.3 %shard_map.104 = (f32[3,64,32,128]{3,2,1,0:T(8,128)}, f32[3,128]{1,0:T(4,128)}) custom-call(f32[3,64,32,128]{3,2,1,0:T(8,128)} %vel_hbm.1, f32[3,32,128]{2,1,0:T(8,128)} %inflow_ref.1, f32[32]{0:T(128)} %az_ref.1, s32[2,32]{1,0:T(2,128)} %bitcast.5, s32[6,32]{1,0:T(8,128)} %bitcast.4, f32[3,128]{1,0:T(4,128)} %lag_ref.1, f32[3,128]{1,0:T(4,128)} %rate_ref.1, ...), custom_call_target="tpu_custom_call" | custom-call | flops 50000000 | bytes 6291456 | tf_op jit(solution)/shard_map/pallas_call | solution.py:420
  30.0 0.0 copy-start
  30.0 3.9 %copy.13 = f32[3,64,32,128]{3,2,1,0:T(8,128)} copy(f32[3,64,32,128]{3,2,1,0:T(8,128)} %get-tuple-element.4) | data formatting | bytes 6291456
  33.8 0.0 copy-done
  33.9 0.6 %copy.14 = f32[3,128]{1,0:T(4,128)} copy(f32[3,128]{1,0:T(4,128)S(1)} %copy-done) | data formatting | bytes 3072
Async XLA Ops:
  30.0 3.9 %copy-start = (f32[3,128]{1,0:T(4,128)S(1)}, f32[3,128]{1,0:T(4,128)}, u32[]{:S(2)}) copy-start(f32[3,128]{1,0:T(4,128)} %get-tuple-element.5) | copy-start | bytes 4612

commit v3 on v2

--- a/solution.py
+++ b/solution.py
@@ -60,6 +60,16 @@
     nx,
     ny,
     vel_hbm,
+    inflow_hbm,
+    az_hbm,
+    pos_hbm,
+    cross_hbm,
+    lag_hbm,
+    rate_hbm,
+    chord_hbm,
+    twist_hbm,
+    out_hbm,
+    state_hbm,
     inflow_ref,
     az_ref,
     pos_ref,
@@ -68,8 +78,8 @@
     rate_ref,
     chord_ref,
     twist_ref,
-    out_hbm,
     state_ref,
+    small_sem,
     grid0,
     grid1,
     grid2,
@@ -103,7 +113,7 @@
     grids = (grid0, grid1, grid2)
     _, cx2, cy, nz = grid0.shape
     cx = cx2 - 2
-    split = cx // 2
+    split = cx * 3 // 4
     total_y = cy * ny
     gx = lax.axis_index("gx")
     gy = lax.axis_index("gy")
@@ -114,6 +124,23 @@
     down = lax.rem(gy + ny - 1, ny)
 
     load = pltpu.make_async_copy(vel_hbm, grid0.at[:, pl.ds(1, cx)], load_sem)
+    smalls = [
+        pltpu.make_async_copy(source, target, small_sem.at[i])
+        for i, (source, target) in enumerate(
+            (
+                (az_hbm, az_ref),
+                (pos_hbm, pos_ref),
+                (cross_hbm, cross_ref),
+                (lag_hbm, lag_ref),
+                (rate_hbm, rate_ref),
+                (chord_hbm, chord_ref),
+                (twist_hbm, twist_ref),
+                (inflow_hbm, inflow_ref),
+            )
+        )
+    ]
+    for copy in smalls:
+        copy.start()
     load.start()
 
     barrier = pltpu.get_barrier_semaphore()
@@ -125,6 +152,9 @@
         pl.semaphore_signal(
             barrier, inc=1, device_id={"gx": lax.rem(gx + d, nx)}, device_id_type=MESH
         )
+
+    for copy in smalls:
+        copy.wait()
 
     rotor, hub_x, load_x, shift_y, valid, az = [], [], [], [], [], []
     for e in range(ENTRIES):
@@ -231,11 +261,6 @@
     stores = []
     for n in range(STEPS):
         src, dst = grids[n], grids[n + 1]
-        halo_copies = [
-            send(src.at[:, cx], halo_x.at[n, 0], hx_send.at[n, 0], hx_recv.at[n, 0], "gx", east),
-            send(src.at[:, 1], halo_x.at[n, 1], hx_send.at[n, 1], hx_recv.at[n, 1], "gx", west),
-        ]
-
         sampled = [[], [], []]
         for e in range(ENTRIES):
             field = None
@@ -257,6 +282,11 @@
             send(part_out.at[n], part_in.at[n, 0], ps_send.at[n, 0], ps_recv.at[n, 0], "gy", up),
             send(part_out.at[n], part_in.at[n, 1], ps_send.at[n, 1], ps_recv.at[n, 1], "gy", down),
         ]
+        halo_copies = [
+            send(src.at[:, cx], halo_x.at[n, 0], hx_send.at[n, 0], hx_recv.at[n, 0], "gx", east),
+            send(src.at[:, 1], halo_x.at[n, 1], hx_send.at[n, 1], hx_recv.at[n, 1], "gx", west),
+        ]
+
         flat = src.reshape(3 * cx2 * cy, nz)
         for c in range(3):
             start = (c * cx2 + 1) * cy
@@ -397,8 +427,11 @@
     block = end_g2[home_x, home_y]
     in_first = cross_ref[0, home_x * ny + home_y] == BLADES * tile
     state_ref[...] = jnp.where(in_first, block[0:BLADES], block[BLADES : 2 * BLADES])
+    last = pltpu.make_async_copy(state_ref, state_hbm, small_sem.at[8])
+    last.start()
     for copy in started:
         copy.wait_send()
+    last.wait()
     for copy in stores:
         copy.wait()
 
@@ -414,8 +447,6 @@
     f32 = jnp.float32
     grid = pltpu.VMEM((3, cx + 2, cy, nz), f32)
     dma = pltpu.SemaphoreType.DMA
-    vmem = pl.BlockSpec(memory_space=pltpu.VMEM)
-    smem = pl.BlockSpec(memory_space=pltpu.SMEM)
     hbm = pl.BlockSpec(memory_space=pl.ANY)
     return pl.pallas_call(
         functools.partial(farm_kernel, nx, ny),
@@ -423,9 +454,19 @@
             jax.ShapeDtypeStruct(velocity.shape, f32),
             jax.ShapeDtypeStruct(lag_state.shape, f32),
         ),
-        in_specs=[hbm, vmem, smem, smem, smem, vmem, vmem, vmem, vmem],
-        out_specs=(hbm, vmem),
+        in_specs=[hbm] * 9,
+        out_specs=(hbm, hbm),
         scratch_shapes=[
+            pltpu.VMEM(inflow.shape, f32),
+            pltpu.SMEM(azimuth.shape, f32),
+            pltpu.SMEM(positions.shape[::-1], jnp.int32),
+            pltpu.SMEM(crossings.shape[::-1], jnp.int32),
+            pltpu.VMEM(lag_state.shape, f32),
+            pltpu.VMEM(lag_state.shape, f32),
+            pltpu.VMEM((1, sections), f32),
+            pltpu.VMEM((1, sections), f32),
+            pltpu.VMEM(lag_state.shape, f32),
+            dma((9,)),
             grid,
             grid,
             grid,

time: 34.6 us -> 33.1 us (0.957)
  Pallas kernels: 29.3 us -> 27.9 us
    pallas_call x1, Pallas kernels: 29.3 us -> 27.9 us  [per_device(): pl.pallas_call(functools.partial(farm_kernel, nx, ny), out_shape=(jax.Sha...]
where the time goes in v3:
time: 33.1 us; the launch traced here: 33 us
  Pallas kernels  27.9 us (84%)
  local copies, waits for them, and re-layouts  4.44 us (13%)
  between operations  0.65 us (2%)
    pallas_call x1, Pallas kernels, per_device(): pl.pallas_call(functools.partial(farm_kernel, nx, ny), out_shape=(jax.Sha...  27.9 us
    unnamed x4, local copies, waits for them, and re-layouts  4.44 us

profile of v3, /device:TPU:0, one launch (start us, length us, event | category | flops | bytes accessed | tf_op | source)
XLA Modules:
  0.0 33.0 jit_solution(3960936454713770109)
XLA Ops:
  0.6 27.9 %shard_map.104 = (f32[3,64,32,128]{3,2,1,0:T(8,128)}, f32[3,128]{1,0:T(4,128)}) custom-call(f32[3,64,32,128]{3,2,1,0:T(8,128)} %vel_hbm.1, f32[3,32,128]{2,1,0:T(8,128)} %inflow_hbm.1, f32[32]{0:T(128)} %az_hbm.1, s32[2,32]{1,0:T(2,128)} %bitcast.5, s32[6,32]{1,0:T(8,128)} %bitcast.4, f32[3,128]{1,0:T(4,128)} %lag_hbm.1, f32[3,128]{1,0:T(4,128)} %rate_hbm.1, ...), custom_call_target="tpu_custom_call" | custom-call | flops 50000000 | bytes 6291456 | tf_op jit(solution)/shard_map/pallas_call | solution.py:451
  28.5 0.0 copy-start
  28.5 3.9 %copy.13 = f32[3,64,32,128]{3,2,1,0:T(8,128)} copy(f32[3,64,32,128]{3,2,1,0:T(8,128)} %get-tuple-element.4) | data formatting | bytes 6291456
  32.4 0.0 copy-done
  32.4 0.6 %copy.14 = f32[3,128]{1,0:T(4,128)} copy(f32[3,128]{1,0:T(4,128)S(1)} %copy-done) | data formatting | bytes 3072
Async XLA Ops:
  28.5 3.9 %copy-start = (f32[3,128]{1,0:T(4,128)S(1)}, f32[3,128]{1,0:T(4,128)}, u32[]{:S(2)}) copy-start(f32[3,128]{1,0:T(4,128)} %get-tuple-element.5) | copy-start | bytes 4612
